TPU v7x, 32 devices: a whole 2x2x4 slice. The times are simulated.
32 devices in a mesh: run: 2 (over y), tile: 4 (over z), site: 2 (over x), freq: 2 (over core).
Axes of the slice: x: 2, y: 2, z: 4, core: 2. Of those that a mesh axis runs over, the one named last changes fastest.
Arguments:
- jacobian: bfloat16 [256, 16, 8, 8, 128], P(('run', 'tile', 'site'), None, 'freq'), parts along dimension 0, may hold values from -6 to 6
- footprint: int32 [256, 16], P(('run', 'tile', 'site')), parts along dimension 0, may hold values from 0 to 4095, as said below
- home: int32 [8192], P('run'), parts along dimension 0, may hold values from 0 to 4095, as said below
- residual: float32 [256, 8, 8], P(('run', 'tile', 'site'), 'freq'), parts along dimension 0, may hold values from -6 to 6
- weights: float32 [256], P(('run', 'tile', 'site')), parts along dimension 0, may hold values from 0.2 to 2
- damping: float32 [8192, 128], P(('run', 'tile', 'site')), parts along dimension 0, may hold values from 2 to 50
- step_lengths: float32 [8], replicated, may hold values from 0.2 to 1.2
Outputs:
- model_step: float32 [8192, 128], P(('run', 'tile', 'site')), parts along dimension 0
- change: float32 [256, 8, 8], P(('run', 'tile', 'site'), 'freq'), parts along dimension 0
- curve: float32 [16, 8], P(('run', 'freq')), parts along dimension 0
There are 2 independent parts, one for each index of `run`. A program takes and returns all parts, laid end to end along the dimension named above; an argument that names none is the same for every part. Nothing has to cross between parts.
Inputs may be any that keep to these rules, and one draw needn't show every extreme that they name: home is a permutation of 0 to 4095. `footprint`: of the 256 entries of each aligned block of 16 sites, at most 64 have home[block] // 512 equal to any one value; one value receives exactly 64 entries from every such block.
All inputs are finite; a program needn't handle non-finite values.
Results may differ from a plain program's by a relative error of at most 0.0029.
Values may be sent and summed in bfloat16 or wider, within the bound.
A program may use at most 64 MiB of HBM per device.

v0:
```python
import jax
import jax.numpy as jnp
from jax import lax
from jax.sharding import PartitionSpec as P


def shards(jacobian, footprint, home, residual, weights, damping, step_lengths):
    site_count, foot_count, freq_local, comps, width = jacobian.shape
    blocks_dev = damping.shape[0]
    tiles = lax.axis_size("tile")
    groups = lax.axis_size("site")
    owner_count = tiles * groups
    entries = site_count * foot_count
    capacity = 2 * entries // owner_count
    weighted = (weights[:, None, None] * residual).astype(jnp.bfloat16)
    grad_terms = jnp.einsum(
        "skfcb,sfc->skb", jacobian, weighted, preferred_element_type=jnp.float32
    )
    curve_terms = weights[:, None, None] * jnp.sum(
        jnp.square(jacobian.astype(jnp.float32)), axis=(2, 3)
    )
    terms = jnp.concatenate([grad_terms, curve_terms], axis=-1).reshape(entries, 2 * width)
    position = home[footprint.reshape(-1)]
    dest_rank = position // blocks_dev
    local_slot = position % blocks_dev
    member = (dest_rank[:, None] == jnp.arange(owner_count, dtype=jnp.int32)[None, :]).astype(
        jnp.int32
    )
    earlier = jnp.cumsum(member, axis=0) - member
    order_in = jnp.sum(earlier * member, axis=1)
    bucket = dest_rank * capacity + order_in
    outgoing = jnp.zeros((owner_count * capacity, 2 * width), jnp.float32).at[bucket].set(terms)
    out_slots = (
        jnp.full((owner_count * capacity,), blocks_dev, jnp.int32).at[bucket].set(local_slot)
    )
    received, in_slots = (
        lax.all_to_all(
            outgoing.reshape(owner_count, capacity, 2 * width),
            ("tile", "site"),
            split_axis=0,
            concat_axis=0,
            tiled=True,
        ),
        lax.all_to_all(
            out_slots.reshape(owner_count, capacity),
            ("tile", "site"),
            split_axis=0,
            concat_axis=0,
            tiled=True,
        ),
    )
    flat_slots = in_slots.reshape(-1)
    totals = jax.ops.segment_sum(
        received.reshape(-1, 2 * width), flat_slots, num_segments=blocks_dev + 1
    )[:blocks_dev]
    totals = lax.psum(totals, "freq")
    model_step = totals[:, :width] / (totals[:, width:] + damping)
    step_low = jnp.concatenate(
        [model_step.astype(jnp.bfloat16), jnp.zeros((1, width), jnp.bfloat16)], axis=0
    )
    reply = step_low[flat_slots]
    returned = lax.all_to_all(
        reply.reshape(owner_count, capacity, width),
        ("tile", "site"),
        split_axis=0,
        concat_axis=0,
        tiled=True,
    )
    entry_rows = returned.reshape(owner_count * capacity, width)[bucket]
    entry_step = entry_rows.reshape(site_count, foot_count, width)
    change = jnp.einsum("skfcb,skb->sfc", jacobian, entry_step, preferred_element_type=jnp.float32)
    scale_total = site_count * owner_count * comps
    gap = residual[:, :, :, None] - step_lengths[None, None, None, :] * change[:, :, :, None]
    partial_sum = jnp.einsum("s,sfca->fa", weights, gap * gap)
    curve = lax.psum(partial_sum, ("tile", "site")) / scale_total
    return (model_step, change, curve)


def solution(mesh):
    placed = (
        P(("run", "tile", "site"), None, "freq", None, None),
        P(("run", "tile", "site"), None),
        P("run"),
        P(("run", "tile", "site"), "freq", None),
        P(("run", "tile", "site")),
        P(("run", "tile", "site"), None),
        P(),
    )
    return jax.shard_map(
        shards,
        mesh=mesh,
        in_specs=placed,
        out_specs=(
            P(("run", "tile", "site"), None),
            P(("run", "tile", "site"), "freq", None),
            P(("run", "freq"), None),
        ),
        check_vma=False,
    )
```

profile of v0, /device:TPU:0, one launch (start us, length us, event | category | flops | bytes accessed | tf_op | source)
XLA Modules:
  0.0 117.0 jit_solution(13052791357690887810)
XLA Ops:
  7.2 0.0 copy-start
  7.2 0.0 copy-start.1
  7.2 0.0 copy-start.5
  7.2 0.0 copy-start.4
  7.2 0.9 reshape.181
  8.2 0.0 copy-done
  8.2 1.7 %gather_fusion = s32[256]{0:T(256)S(1)} fusion(s32[4096]{0:T(1024)S(1)} %copy-done, s32[1024]{0:T(1024)S(1)} %pad_clamp_fusion.2), kind=kCustom, calls=%fused_computation | custom fusion | bytes 3072 | tf_op jit(solution)/shard_map/gather | solution.py:23
  9.9 0.6 reduce-window.6
  10.5 0.2 slice_reduce_fusion
  10.8 0.1 fusion.10
  10.9 1.4 %scatter_custom_fusion = s32[512]{0:T(512)S(1)} fusion(s32[256]{0:T(256)S(1)} %bitcast.64, s32[256]{0:T(256)S(1)} %get-tuple-element.5, s32[]{:T(128)} %constant.41.clone.1), kind=kCustom, calls=%fused_computation.49 | custom fusion | bytes 2052 | tf_op jit(solution)/shard_map/scatter | solution.py:34
  12.3 0.7 all_to_all.12
  13.0 7.3 %all-to-all-start = ((s32[8,1,64]{2,1,0:T(1,128)}), s32[8,1,64]{2,1,0:T(1,128)S(1)}, u32[]{:S(2)}, u32[]{:S(2)}) async-start(s32[8,1,64]{2,1,0:T(1,128)} %all_to_all.12), calls=%async_computation | async-start | bytes 8192 | tf_op jit(solution)/shard_map/all_to_all | solution.py:44
  20.2 2.3 %multiply_reduce_fusion = f32[16,16,128]{2,1,0:T(8,128)S(1)} fusion(bf16[16,16,4,8,128]{4,3,2,1,0:T(8,128)(2,1)} %param.7), kind=kLoop, calls=%fused_computation.6 | loop fusion | flops 3112960 | bytes 2228224 | tf_op jit(solution)/shard_map/reduce_sum | solution.py:19
  22.6 0.0 copy-done.5
  22.6 0.1 broadcast_multiply_fusion
  22.7 0.0 copy-done.4
  22.7 0.1 copy.14
  22.8 0.0 copy-done.1
  22.8 0.6 fusion.22
  23.4 0.0 copy-start.2
  23.4 2.2 %scatter_custom_fusion.1 = f32[512,256]{1,0:T(8,128)} fusion(s32[256]{0:T(256)S(1)} %bitcast.65, f32[256,256]{1,0:T(8,128)S(1)} %bitcast.56, f32[]{:T(128)} %constant.40.clone.1), kind=kCustom, calls=%fused_computation.14 | custom fusion | bytes 524292 | tf_op jit(solution)/shard_map/scatter | solution.py:32
  25.6 1.0 all-to-all-done
  26.6 5.0 %all-to-all-start.1 = ((f32[8,64,256]{2,1,0:T(8,128)}), f32[8,64,256]{2,1,0:T(8,128)S(1)}, u32[]{:S(2)}, u32[]{:S(2)}) async-start(f32[8,64,256]{2,1,0:T(8,128)} %bitcast.11), calls=%async_computation.1 | async-start | bytes 1048576 | tf_op jit(solution)/shard_map/all_to_all | solution.py:37
  31.6 0.0 all-reduce.3.cloned.1.call-start
  31.7 0.5 broadcast.204
  32.2 0.7 reduce.7
  32.8 0.1 reshape.231
  32.9 12.7 %all-to-all-done.1 = f32[8,64,256]{2,1,0:T(8,128)S(1)} async-done(((f32[8,64,256]{2,1,0:T(8,128)}), f32[8,64,256]{2,1,0:T(8,128)S(1)}, u32[]{:S(2)}, u32[]{:S(2)}) %all-to-all-start.1) | async-done | bytes 524320 | tf_op jit(solution)/shard_map/all_to_all | solution.py:37
  45.6 3.7 %scatter_custom_fusion.2 = f32[513,256]{1,0:T(8,128)S(1)} fusion(s32[512]{0:T(512)S(1)} %reshape.231, f32[512,256]{1,0:T(8,128)S(1)} %bitcast.54, f32[]{:T(128)} %constant.40.clone.1), kind=kCustom, calls=%fused_computation.9 | custom fusion | flops 131072 | bytes 525316 | tf_op jit(solution)/shard_map/scatter-add | solution.py:53
  49.3 0.8 slice.27
  50.1 0.0 all-reduce.3.cloned.1.call-update
  50.1 0.1 broadcast_in_dim_reshape.3
  50.2 17.9 %all-reduce.3.cloned.1.call-done = f32[512,256]{1,0:T(8,128)} async-done(((f32[512,256]{1,0:T(8,128)}), f32[512,256]{1,0:T(8,128)}) %all-reduce.3.cloned.1.call-update) | async-done | bytes 524304 | tf_op jit(solution)/shard_map/psum | solution.py:56
  68.1 0.0 copy-done.2
  68.1 1.8 %fusion.17 = (bf16[512,128]{1,0:T(8,128)(2,1)S(1)}, f32[512,128]{1,0:T(8,128)}) fusion(f32[512,128]{1,0:T(8,128)S(1)} %copy-done.2, f32[512,256]{1,0:T(8,128)} %all-reduce.3.cloned.1.call-done), kind=kLoop, calls=%fused_computation.55 | loop fusion | flops 196608 | bytes 1179648 | tf_op jit(solution)/shard_map/convert_element_type | solution.py:59
  69.9 1.9 %gather_fusion.1 = bf16[512,128]{1,0:T(8,128)(2,1)} fusion(bf16[513,128]{1,0:T(8,128)(2,1)S(1)} %concatenate.7, s32[1024]{0:T(1024)S(1)} %pad_clamp_fusion.1), kind=kCustom, calls=%fused_computation.1 | custom fusion | bytes 264192 | tf_op jit(solution)/shard_map/gather | solution.py:61
  71.8 5.8 %all-to-all-start.2 = ((bf16[8,64,128]{2,1,0:T(8,128)(2,1)}), bf16[8,64,128]{2,1,0:T(8,128)(2,1)S(1)}, u32[]{:S(2)}, u32[]{:S(2)}) async-start(bf16[8,64,128]{2,1,0:T(8,128)(2,1)} %bitcast.14), calls=%async_computation.2 | async-start | bytes 262144 | tf_op jit(solution)/shard_map/all_to_all | solution.py:62
  77.6 7.4 %all-to-all-done.2 = bf16[8,64,128]{2,1,0:T(8,128)(2,1)S(1)} async-done(((bf16[8,64,128]{2,1,0:T(8,128)(2,1)}), bf16[8,64,128]{2,1,0:T(8,128)(2,1)S(1)}, u32[]{:S(2)}, u32[]{:S(2)}) %all-to-all-start.2) | async-done | bytes 131104 | tf_op jit(solution)/shard_map/all_to_all | solution.py:62
  85.1 0.0 copy-start.6
  85.1 0.9 gather_fusion.2
  85.9 4.7 %fusion = f32[16,1,4,8,1]{3,1,4,2,0:T(1,128)S(1)} fusion(bf16[16,16,4,8,128]{4,3,2,1,0:T(8,128)(2,1)S(1)} %copy-done.1, bf16[16,16,128,1,1]{2,1,0,3,4:T(8,128)(2,1)S(1)} %bitcast.57), kind=kOutput, calls=%fused_computation.7 | convolution fusion | flops 2097152 | bytes 2164736 | tf_op jit(solution)/shard_map/skfcb,skb->sfc/dot_general | solution.py:71
  90.6 0.1 copy.18
  90.7 0.0 copy-start.3
  90.7 0.0 copy-done.6
  90.7 0.1 multiply_reduce_fusion.1
  90.8 0.1 fusion.19
  91.0 18.6 %psum.15 = f32[4,8]{1,0:T(4,128)S(1)} all-reduce(f32[4,8]{1,0:T(4,128)S(1)} %bitcast.63), channel_id=1, replica_groups=mesh['run'=2,'tile'=4,'site'=2,'freq'=2] {'tile','site'}, use_global_device_ids=true, to_apply=%region_9.10 | all-reduce | flops 32 | bytes 256 | tf_op jit(solution)/shard_map/psum | solution.py:75
  109.5 0.6 broadcast_multiply_fusion.1
  110.1 0.0 copy-done.3
  (14 shorter events, 0.2 us)
Async XLA Ops:
  7.2 1.0 copy-start
  7.2 15.6 %copy-start.1 = (bf16[16,16,4,8,128]{4,3,2,1,0:T(8,128)(2,1)S(1)}, bf16[16,16,4,8,128]{4,3,2,1,0:T(8,128)(2,1)}, u32[]{:S(2)}) copy-start(bf16[16,16,4,8,128]{4,3,2,1,0:T(8,128)(2,1)} %param.7) | copy-start | bytes 6291460
  7.2 15.4 %copy-start.5 = (f32[16]{0:T(128)S(1)}, f32[16]{0:T(128)}, u32[]{:S(2)}) copy-start(f32[16]{0:T(128)} %param.11) | copy-start | bytes 196
  7.2 15.5 %copy-start.4 = (f32[16,4,8]{0,2,1:T(8,128)S(1)}, f32[16,4,8]{0,2,1:T(8,128)}, u32[]{:S(2)}) copy-start(f32[16,4,8]{0,2,1:T(8,128)} %param.10) | copy-start | bytes 6148
  13.0 13.6 %all-to-all-start = ((s32[8,1,64]{2,1,0:T(1,128)}), s32[8,1,64]{2,1,0:T(1,128)S(1)}, u32[]{:S(2)}, u32[]{:S(2)}) async-start(s32[8,1,64]{2,1,0:T(1,128)} %all_to_all.12), calls=%async_computation | async-start | bytes 8192 | tf_op jit(solution)/shard_map/all_to_all | solution.py:44
  23.4 44.7 %copy-start.2 = (f32[512,128]{1,0:T(8,128)S(1)}, f32[512,128]{1,0:T(8,128)}, u32[]{:S(2)}) copy-start(f32[512,128]{1,0:T(8,128)} %param.12) | copy-start | bytes 786436
  26.6 19.0 %all-to-all-start.1 = ((f32[8,64,256]{2,1,0:T(8,128)}), f32[8,64,256]{2,1,0:T(8,128)S(1)}, u32[]{:S(2)}, u32[]{:S(2)}) async-start(f32[8,64,256]{2,1,0:T(8,128)} %bitcast.11), calls=%async_computation.1 | async-start | bytes 1048576 | tf_op jit(solution)/shard_map/all_to_all | solution.py:37
  31.6 36.5 %all-reduce.3.cloned.1.call-start = ((), (), s32[]{:S(2)}) async-start(), calls=%async_computation.3 | async-start | bytes 1048576 | tf_op jit(solution)/shard_map/psum | solution.py:56
  71.8 13.2 %all-to-all-start.2 = ((bf16[8,64,128]{2,1,0:T(8,128)(2,1)}), bf16[8,64,128]{2,1,0:T(8,128)(2,1)S(1)}, u32[]{:S(2)}, u32[]{:S(2)}) async-start(bf16[8,64,128]{2,1,0:T(8,128)(2,1)} %bitcast.14), calls=%async_computation.2 | async-start | bytes 262144 | tf_op jit(solution)/shard_map/all_to_all | solution.py:62
  85.1 5.6 %copy-start.6 = (f32[8]{0:T(128)S(1)}, f32[8]{0:T(128)}, u32[]{:S(2)}) copy-start(f32[8]{0:T(128)} %param.13) | copy-start | bytes 100
  90.7 19.4 %copy-start.3 = (f32[16,1,4,8,1]{0,3,2,1,4:T(8,128)}, f32[16,1,4,8,1]{0,3,2,1,4:T(8,128)S(1)}, u32[]{:S(2)}) copy-start(f32[16,1,4,8,1]{0,3,2,1,4:T(8,128)S(1)} %copy.18) | copy-start | bytes 6148
Sparse Core Ops, SparseCore 0:
  50.3 17.8 all-reduce.2
where the time goes:
time: 117 us
  waiting for transfers between devices  39 us (33%)
  blocking collectives  18.6 us (16%)
  starting transfers between devices  18.1 us (15%)
  between operations  14.2 us (12%)
  local copies, waits for them, and re-layouts  11.6 us (10%)
  other arithmetic  10.1 us (9%)
  matrix products  5.41 us (5%)
    psum x1, blocking collectives, shards(): curve = lax.psum(partial_sum, ('tile', 'site')) / scale_total  18.6 us
    psum x1, waiting for transfers between devices, shards(): totals = lax.psum(totals, 'freq')  17.9 us
    all_to_all x1, waiting for transfers between devices, shards(): lax.all_to_all(outgoing.reshape(owner_count, capacity, 2 * width), ('tile...  12.7 us
    all_to_all x1, waiting for transfers between devices, shards(): lax.all_to_all(reply.reshape(owner_count, capacity, width), ('tile', 'sit...  7.43 us
    all_to_all x1, starting transfers between devices, shards(): lax.all_to_all(out_slots.reshape(owner_count, capacity), ('tile', 'site')...  7.25 us
    all_to_all x1, starting transfers between devices, shards(): lax.all_to_all(reply.reshape(owner_count, capacity, width), ('tile', 'sit...  5.78 us
    all_to_all x1, starting transfers between devices, shards(): lax.all_to_all(outgoing.reshape(owner_count, capacity, 2 * width), ('tile...  5 us
    dot_general x1, matrix products, shards(): jnp.einsum('skfcb,skb->sfc', jacobian, entry_step, preferred_element_type...  4.69 us
  transfers between devices with their start and end apart: 4, of which 4 were waited for; matrix products, arithmetic and copies ran while one was open for 6% of the time, Pallas kernels for 0%

commit v1 on v0

--- a/solution.py
+++ b/solution.py
@@ -2,6 +2,22 @@
 import jax.numpy as jnp
 from jax import lax
 from jax.sharding import PartitionSpec as P
+
+
+def exchange_in_pairs(x, axis, split, join):
+    ways, here = (lax.axis_size(axis), lax.axis_index(axis))
+    width = x.shape[split] // ways
+    dims = list(x.shape)
+    dims[split] = width
+    height = dims[join]
+    dims[join] = height * ways
+    full = jnp.zeros(dims, x.dtype)
+    for mask in range(ways):
+        part = lax.dynamic_slice_in_dim(x, (here ^ mask) * width, width, axis=split)
+        if mask:
+            part = lax.ppermute(part, axis, [(d, d ^ mask) for d in range(ways)])
+        full = lax.dynamic_update_slice_in_dim(full, part, (here ^ mask) * height, axis=join)
+    return full
 
 
 def shards(jacobian, footprint, home, residual, weights, damping, step_lengths):
@@ -59,12 +75,8 @@
         [model_step.astype(jnp.bfloat16), jnp.zeros((1, width), jnp.bfloat16)], axis=0
     )
     reply = step_low[flat_slots]
-    returned = lax.all_to_all(
-        reply.reshape(owner_count, capacity, width),
-        ("tile", "site"),
-        split_axis=0,
-        concat_axis=0,
-        tiled=True,
+    returned = exchange_in_pairs(
+        reply.reshape(owner_count, capacity, width), ("tile", "site"), 0, 0
     )
     entry_rows = returned.reshape(owner_count * capacity, width)[bucket]
     entry_step = entry_rows.reshape(site_count, foot_count, width)

time: 117 us -> 120 us (1.026)
  starting transfers between devices: 18.1 us -> 23.5 us
  waiting for transfers between devices: 39 us -> 37.7 us
    ppermute x0 -> x7, starting transfers between devices: none -> 11.2 us  [exchange_in_pairs(): part = lax.ppermute(part, axis, [(d, d ^ mask) for d in range(ways)])]
    all_to_all x1 -> x0, waiting for transfers between devices: 7.43 us -> none  [shards(): lax.all_to_all(reply.reshape(owner_count, capacity, width), ('tile', 'sit...]
    ppermute x0 -> x7, waiting for transfers between devices: none -> 6.17 us  [exchange_in_pairs(): part = lax.ppermute(part, axis, [(d, d ^ mask) for d in range(ways)])]
    all_to_all x1 -> x0, starting transfers between devices: 5.78 us -> none  [shards(): lax.all_to_all(reply.reshape(owner_count, capacity, width), ('tile', 'sit...]
  transfers between devices with their start and end apart: 4 -> 10, of which waited for: 4 -> 6; matrix products, arithmetic and copies ran while one was open for 6% -> 6% of each run, Pallas kernels for 0% -> 0%
where the time goes in v1:
time: 120 us
  waiting for transfers between devices  37.7 us (31%)
  starting transfers between devices  23.5 us (20%)
  blocking collectives  17.7 us (15%)
  between operations  14.3 us (12%)
  local copies, waits for them, and re-layouts  11.2 us (9%)
  other arithmetic  10.1 us (8%)
  matrix products  5.41 us (5%)
    psum x1, waiting for transfers between devices, shards(): totals = lax.psum(totals, 'freq')  17.9 us
    psum x1, blocking collectives, shards(): curve = lax.psum(partial_sum, ('tile', 'site')) / scale_total  17.7 us
    all_to_all x1, waiting for transfers between devices, shards(): lax.all_to_all(outgoing.reshape(owner_count, capacity, 2 * width), ('tile...  12.7 us
    ppermute x7, starting transfers between devices, exchange_in_pairs(): part = lax.ppermute(part, axis, [(d, d ^ mask) for d in range(ways)])  11.2 us
    all_to_all x1, starting transfers between devices, shards(): lax.all_to_all(out_slots.reshape(owner_count, capacity), ('tile', 'site')...  7.25 us
    ppermute x7, waiting for transfers between devices, exchange_in_pairs(): part = lax.ppermute(part, axis, [(d, d ^ mask) for d in range(ways)])  6.17 us
    all_to_all x1, starting transfers between devices, shards(): lax.all_to_all(outgoing.reshape(owner_count, capacity, 2 * width), ('tile...  5 us
    dot_general x1, matrix products, shards(): jnp.einsum('skfcb,skb->sfc', jacobian, entry_step, preferred_element_type...  4.69 us
  transfers between devices with their start and end apart: 10, of which 6 were waited for; matrix products, arithmetic and copies ran while one was open for 6% of the time, Pallas kernels for 0%

profile of v1, /device:TPU:0, one launch (start us, length us, event | category | flops | bytes accessed | tf_op | source)
XLA Modules:
  0.0 119.8 jit_solution(16791874342603576307)
XLA Ops:
  7.2 0.0 copy-start
  7.2 0.0 copy-start.1
  7.2 0.0 copy-start.5
  7.2 0.0 copy-start.4
  7.2 0.9 reshape.181
  8.2 0.0 copy-done
  8.2 1.7 %gather_fusion = s32[256]{0:T(256)S(1)} fusion(s32[4096]{0:T(1024)S(1)} %copy-done, s32[1024]{0:T(1024)S(1)} %pad_clamp_fusion.2), kind=kCustom, calls=%fused_computation | custom fusion | bytes 3072 | tf_op jit(solution)/shard_map/gather | solution.py:39
  9.9 0.6 reduce-window.6
  10.5 0.2 slice_reduce_fusion
  10.8 0.1 fusion.10
  10.9 1.4 %scatter_custom_fusion = s32[512]{0:T(512)S(1)} fusion(s32[256]{0:T(256)S(1)} %bitcast.65, s32[256]{0:T(256)S(1)} %get-tuple-element.13, s32[]{:T(128)} %constant.25.clone.1), kind=kCustom, calls=%fused_computation.64 | custom fusion | bytes 2052 | tf_op jit(solution)/shard_map/scatter | solution.py:50
  12.3 0.7 all_to_all.9
  13.0 7.3 %all-to-all-start = ((s32[8,1,64]{2,1,0:T(1,128)}), s32[8,1,64]{2,1,0:T(1,128)S(1)}, u32[]{:S(2)}, u32[]{:S(2)}) async-start(s32[8,1,64]{2,1,0:T(1,128)} %all_to_all.9), calls=%async_computation | async-start | bytes 8192 | tf_op jit(solution)/shard_map/all_to_all | solution.py:60
  20.2 2.3 %multiply_reduce_fusion = f32[16,16,128]{2,1,0:T(8,128)S(1)} fusion(bf16[16,16,4,8,128]{4,3,2,1,0:T(8,128)(2,1)} %param.7), kind=kLoop, calls=%fused_computation.6 | loop fusion | flops 3112960 | bytes 2228224 | tf_op jit(solution)/shard_map/reduce_sum | solution.py:35
  22.6 0.0 copy-done.5
  22.6 0.1 broadcast_multiply_fusion
  22.7 0.0 copy-done.4
  22.7 0.1 copy.14
  22.8 0.0 copy-done.1
  22.8 0.6 fusion.22
  23.4 0.0 copy-start.2
  23.4 2.2 %scatter_custom_fusion.1 = f32[512,256]{1,0:T(8,128)} fusion(s32[256]{0:T(256)S(1)} %bitcast.66, f32[256,256]{1,0:T(8,128)S(1)} %bitcast.57, f32[]{:T(128)} %constant.24.clone.1), kind=kCustom, calls=%fused_computation.14 | custom fusion | bytes 524292 | tf_op jit(solution)/shard_map/scatter | solution.py:48
  25.6 1.0 all-to-all-done
  26.6 5.0 %all-to-all-start.1 = ((f32[8,64,256]{2,1,0:T(8,128)}), f32[8,64,256]{2,1,0:T(8,128)S(1)}, u32[]{:S(2)}, u32[]{:S(2)}) async-start(f32[8,64,256]{2,1,0:T(8,128)} %bitcast.11), calls=%async_computation.1 | async-start | bytes 1048576 | tf_op jit(solution)/shard_map/all_to_all | solution.py:53
  31.6 0.0 all-reduce.3.cloned.1.call-start
  31.7 0.5 broadcast.216
  32.2 0.7 reduce.7
  32.8 0.1 reshape.231
  32.9 12.7 %all-to-all-done.1 = f32[8,64,256]{2,1,0:T(8,128)S(1)} async-done(((f32[8,64,256]{2,1,0:T(8,128)}), f32[8,64,256]{2,1,0:T(8,128)S(1)}, u32[]{:S(2)}, u32[]{:S(2)}) %all-to-all-start.1) | async-done | bytes 524320 | tf_op jit(solution)/shard_map/all_to_all | solution.py:53
  45.6 3.7 %scatter_custom_fusion.2 = f32[513,256]{1,0:T(8,128)S(1)} fusion(s32[512]{0:T(512)S(1)} %reshape.231, f32[512,256]{1,0:T(8,128)S(1)} %bitcast.55, f32[]{:T(128)} %constant.24.clone.1), kind=kCustom, calls=%fused_computation.9 | custom fusion | flops 131072 | bytes 525316 | tf_op jit(solution)/shard_map/scatter-add | solution.py:69
  49.3 0.8 slice.27
  50.1 0.0 all-reduce.3.cloned.1.call-update
  50.2 0.1 broadcast_in_dim_reshape.3
  50.3 17.9 %all-reduce.3.cloned.1.call-done = f32[512,256]{1,0:T(8,128)} async-done(((f32[512,256]{1,0:T(8,128)}), f32[512,256]{1,0:T(8,128)}) %all-reduce.3.cloned.1.call-update) | async-done | bytes 524304 | tf_op jit(solution)/shard_map/psum | solution.py:72
  68.1 0.0 copy-done.2
  68.1 1.8 %fusion.17 = (bf16[512,128]{1,0:T(8,128)(2,1)S(1)}, f32[512,128]{1,0:T(8,128)}) fusion(f32[512,128]{1,0:T(8,128)S(1)} %copy-done.2, f32[512,256]{1,0:T(8,128)} %all-reduce.3.cloned.1.call-done), kind=kLoop, calls=%fused_computation.70 | loop fusion | flops 196608 | bytes 1179648 | tf_op jit(solution)/shard_map/convert_element_type | solution.py:75
  69.9 1.3 %gather_fusion.1 = bf16[512,128]{1,0:T(8,128)(2,1)S(1)} fusion(bf16[513,128]{1,0:T(8,128)(2,1)S(1)} %concatenate.7, s32[1024]{0:T(1024)S(1)} %pad_clamp_fusion.1), kind=kCustom, calls=%fused_computation.1 | custom fusion | bytes 264192 | tf_op jit(solution)/shard_map/gather | solution.py:77
  71.4 1.8 %collective-permute-start = (bf16[1,64,128]{2,1,0:T(8,128)(2,1)S(1)}, bf16[1,64,128]{2,1,0:T(8,128)(2,1)S(1)}, u32[]{:S(2)}, u32[]{:S(2)}) collective-permute-start(bf16[1,64,128]{2,1,0:T(8,128)(2,1)S(1)} %get-tuple-element.11), channel_id=1, source_target_pairs={{0,2},{2,0},{4,6},{6,4},{8,10},{10,8},{12,14},{14,12},{1,3},{3,1},... | collective-permute-start | bytes 49160 | tf_op jit(solution)/shard_map/ppermute | solution.py:18
  73.2 1.5 %collective-permute-start.1 = (bf16[1,64,128]{2,1,0:T(8,128)(2,1)S(1)}, bf16[1,64,128]{2,1,0:T(8,128)(2,1)S(1)}, u32[]{:S(2)}, u32[]{:S(2)}) collective-permute-start(bf16[1,64,128]{2,1,0:T(8,128)(2,1)S(1)} %get-tuple-element.10), channel_id=1, source_target_pairs={{0,4},{2,6},{4,0},{6,2},{8,12},{10,14},{12,8},{14,10},{1,5},{3,7},... | collective-permute-start | bytes 49160 | tf_op jit(solution)/shard_map/ppermute | solution.py:18
  74.7 0.3 collective-permute-start.2
  74.9 2.7 %collective-permute-start.3 = (bf16[1,64,128]{2,1,0:T(8,128)(2,1)S(1)}, bf16[1,64,128]{2,1,0:T(8,128)(2,1)S(1)}, u32[]{:S(2)}, u32[]{:S(2)}) collective-permute-start(bf16[1,64,128]{2,1,0:T(8,128)(2,1)S(1)} %get-tuple-element.8), channel_id=1, source_target_pairs={{0,8},{2,10},{4,12},{6,14},{8,0},{10,2},{12,4},{14,6},{1,9},{3,11}... | collective-permute-start | bytes 49160 | tf_op jit(solution)/shard_map/ppermute | solution.py:18
  77.6 1.4 %collective-permute-start.4 = (bf16[1,64,128]{2,1,0:T(8,128)(2,1)S(1)}, bf16[1,64,128]{2,1,0:T(8,128)(2,1)S(1)}, u32[]{:S(2)}, u32[]{:S(2)}) collective-permute-start(bf16[1,64,128]{2,1,0:T(8,128)(2,1)S(1)} %get-tuple-element.7), channel_id=1, source_target_pairs={{0,10},{2,8},{4,14},{6,12},{8,2},{10,0},{12,6},{14,4},{1,11},{3,9}... | collective-permute-start | bytes 49160 | tf_op jit(solution)/shard_map/ppermute | solution.py:18
  79.0 0.0 collective-permute-done
  79.0 3.3 %collective-permute-start.5 = (bf16[1,64,128]{2,1,0:T(8,128)(2,1)S(1)}, bf16[1,64,128]{2,1,0:T(8,128)(2,1)S(1)}, u32[]{:S(2)}, u32[]{:S(2)}) collective-permute-start(bf16[1,64,128]{2,1,0:T(8,128)(2,1)S(1)} %get-tuple-element.6), channel_id=1, source_target_pairs={{0,12},{2,14},{4,8},{6,10},{8,4},{10,6},{12,0},{14,2},{1,13},{3,15... | collective-permute-start | bytes 49160 | tf_op jit(solution)/shard_map/ppermute | solution.py:18
  82.4 0.0 collective-permute-done.1
  82.4 0.2 collective-permute-start.6
  82.6 0.0 collective-permute-done.2
  82.6 0.0 collective-permute-done.3
  82.6 0.5 collective-permute-done.4
  83.1 1.4 %collective-permute-done.5 = bf16[1,64,128]{2,1,0:T(8,128)(2,1)S(1)} collective-permute-done((bf16[1,64,128]{2,1,0:T(8,128)(2,1)S(1)}, bf16[1,64,128]{2,1,0:T(8,128)(2,1)S(1)}, u32[]{:S(2)}, u32[]{:S(2)}) %collective-permute-start.5) | collective-permute-done | bytes 16416 | tf_op jit(solution)/shard_map/ppermute | solution.py:18
  84.6 4.2 %collective-permute-done.6 = bf16[1,64,128]{2,1,0:T(8,128)(2,1)S(1)} collective-permute-done((bf16[1,64,128]{2,1,0:T(8,128)(2,1)S(1)}, bf16[1,64,128]{2,1,0:T(8,128)(2,1)S(1)}, u32[]{:S(2)}, u32[]{:S(2)}) %collective-permute-start.6) | collective-permute-done | bytes 16416 | tf_op jit(solution)/shard_map/ppermute | solution.py:18
  88.8 0.0 copy-start.6
  88.8 0.9 gather_fusion.2
  89.7 4.7 %fusion = f32[16,1,4,8,1]{3,1,4,2,0:T(1,128)S(1)} fusion(bf16[16,16,4,8,128]{4,3,2,1,0:T(8,128)(2,1)S(1)} %copy-done.1, bf16[16,16,128,1,1]{2,1,0,3,4:T(8,128)(2,1)S(1)} %bitcast.58), kind=kOutput, calls=%fused_computation.7 | convolution fusion | flops 2097152 | bytes 2164736 | tf_op jit(solution)/shard_map/skfcb,skb->sfc/dot_general | solution.py:83
  94.4 0.1 copy.18
  94.4 0.0 copy-start.3
  94.4 0.0 copy-done.6
  94.4 0.1 multiply_reduce_fusion.1
  94.6 0.1 fusion.19
  94.7 17.7 %psum.15 = f32[4,8]{1,0:T(4,128)S(1)} all-reduce(f32[4,8]{1,0:T(4,128)S(1)} %bitcast.64), channel_id=1, replica_groups=mesh['run'=2,'tile'=4,'site'=2,'freq'=2] {'tile','site'}, use_global_device_ids=true, to_apply=%region_9.10 | all-reduce | flops 32 | bytes 256 | tf_op jit(solution)/shard_map/psum | solution.py:87
  112.4 0.6 broadcast_multiply_fusion.1
  113.0 0.0 copy-done.3
  (23 shorter events, 0.3 us)
Async XLA Ops:
  7.2 1.0 copy-start
  7.2 15.6 %copy-start.1 = (bf16[16,16,4,8,128]{4,3,2,1,0:T(8,128)(2,1)S(1)}, bf16[16,16,4,8,128]{4,3,2,1,0:T(8,128)(2,1)}, u32[]{:S(2)}) copy-start(bf16[16,16,4,8,128]{4,3,2,1,0:T(8,128)(2,1)} %param.7) | copy-start | bytes 6291460
  7.2 15.4 %copy-start.5 = (f32[16]{0:T(128)S(1)}, f32[16]{0:T(128)}, u32[]{:S(2)}) copy-start(f32[16]{0:T(128)} %param.11) | copy-start | bytes 196
  7.2 15.5 %copy-start.4 = (f32[16,4,8]{0,2,1:T(8,128)S(1)}, f32[16,4,8]{0,2,1:T(8,128)}, u32[]{:S(2)}) copy-start(f32[16,4,8]{0,2,1:T(8,128)} %param.10) | copy-start | bytes 6148
  13.0 13.6 %all-to-all-start = ((s32[8,1,64]{2,1,0:T(1,128)}), s32[8,1,64]{2,1,0:T(1,128)S(1)}, u32[]{:S(2)}, u32[]{:S(2)}) async-start(s32[8,1,64]{2,1,0:T(1,128)} %all_to_all.9), calls=%async_computation | async-start | bytes 8192 | tf_op jit(solution)/shard_map/all_to_all | solution.py:60
  23.4 44.7 %copy-start.2 = (f32[512,128]{1,0:T(8,128)S(1)}, f32[512,128]{1,0:T(8,128)}, u32[]{:S(2)}) copy-start(f32[512,128]{1,0:T(8,128)} %param.12) | copy-start | bytes 786436
  26.6 19.0 %all-to-all-start.1 = ((f32[8,64,256]{2,1,0:T(8,128)}), f32[8,64,256]{2,1,0:T(8,128)S(1)}, u32[]{:S(2)}, u32[]{:S(2)}) async-start(f32[8,64,256]{2,1,0:T(8,128)} %bitcast.11), calls=%async_computation.1 | async-start | bytes 1048576 | tf_op jit(solution)/shard_map/all_to_all | solution.py:53
  31.6 36.5 %all-reduce.3.cloned.1.call-start = ((), (), s32[]{:S(2)}) async-start(), calls=%async_computation.2 | async-start | bytes 1048576 | tf_op jit(solution)/shard_map/psum | solution.py:72
  71.4 7.7 %collective-permute-start = (bf16[1,64,128]{2,1,0:T(8,128)(2,1)S(1)}, bf16[1,64,128]{2,1,0:T(8,128)(2,1)S(1)}, u32[]{:S(2)}, u32[]{:S(2)}) collective-permute-start(bf16[1,64,128]{2,1,0:T(8,128)(2,1)S(1)} %get-tuple-element.11), channel_id=1, source_target_pairs={{0,2},{2,0},{4,6},{6,4},{8,10},{10,8},{12,14},{14,12},{1,3},{3,1},... | collective-permute-start | bytes 49160 | tf_op jit(solution)/shard_map/ppermute | solution.py:18
  73.2 9.2 %collective-permute-start.1 = (bf16[1,64,128]{2,1,0:T(8,128)(2,1)S(1)}, bf16[1,64,128]{2,1,0:T(8,128)(2,1)S(1)}, u32[]{:S(2)}, u32[]{:S(2)}) collective-permute-start(bf16[1,64,128]{2,1,0:T(8,128)(2,1)S(1)} %get-tuple-element.10), channel_id=1, source_target_pairs={{0,4},{2,6},{4,0},{6,2},{8,12},{10,14},{12,8},{14,10},{1,5},{3,7},... | collective-permute-start | bytes 49160 | tf_op jit(solution)/shard_map/ppermute | solution.py:18
  74.7 7.9 %collective-permute-start.2 = (bf16[1,64,128]{2,1,0:T(8,128)(2,1)S(1)}, bf16[1,64,128]{2,1,0:T(8,128)(2,1)S(1)}, u32[]{:S(2)}, u32[]{:S(2)}) collective-permute-start(bf16[1,64,128]{2,1,0:T(8,128)(2,1)S(1)} %get-tuple-element.9), channel_id=1, source_target_pairs={{0,6},{2,4},{4,2},{6,0},{8,14},{10,12},{12,10},{14,8},{1,7},{3,5},... | collective-permute-start | bytes 49160 | tf_op jit(solution)/shard_map/ppermute | solution.py:18
  74.9 7.7 %collective-permute-start.3 = (bf16[1,64,128]{2,1,0:T(8,128)(2,1)S(1)}, bf16[1,64,128]{2,1,0:T(8,128)(2,1)S(1)}, u32[]{:S(2)}, u32[]{:S(2)}) collective-permute-start(bf16[1,64,128]{2,1,0:T(8,128)(2,1)S(1)} %get-tuple-element.8), channel_id=1, source_target_pairs={{0,8},{2,10},{4,12},{6,14},{8,0},{10,2},{12,4},{14,6},{1,9},{3,11}... | collective-permute-start | bytes 49160 | tf_op jit(solution)/shard_map/ppermute | solution.py:18
  77.6 5.5 %collective-permute-start.4 = (bf16[1,64,128]{2,1,0:T(8,128)(2,1)S(1)}, bf16[1,64,128]{2,1,0:T(8,128)(2,1)S(1)}, u32[]{:S(2)}, u32[]{:S(2)}) collective-permute-start(bf16[1,64,128]{2,1,0:T(8,128)(2,1)S(1)} %get-tuple-element.7), channel_id=1, source_target_pairs={{0,10},{2,8},{4,14},{6,12},{8,2},{10,0},{12,6},{14,4},{1,11},{3,9}... | collective-permute-start | bytes 49160 | tf_op jit(solution)/shard_map/ppermute | solution.py:18
  79.0 5.5 %collective-permute-start.5 = (bf16[1,64,128]{2,1,0:T(8,128)(2,1)S(1)}, bf16[1,64,128]{2,1,0:T(8,128)(2,1)S(1)}, u32[]{:S(2)}, u32[]{:S(2)}) collective-permute-start(bf16[1,64,128]{2,1,0:T(8,128)(2,1)S(1)} %get-tuple-element.6), channel_id=1, source_target_pairs={{0,12},{2,14},{4,8},{6,10},{8,4},{10,6},{12,0},{14,2},{1,13},{3,15... | collective-permute-start | bytes 49160 | tf_op jit(solution)/shard_map/ppermute | solution.py:18
  82.4 6.4 %collective-permute-start.6 = (bf16[1,64,128]{2,1,0:T(8,128)(2,1)S(1)}, bf16[1,64,128]{2,1,0:T(8,128)(2,1)S(1)}, u32[]{:S(2)}, u32[]{:S(2)}) collective-permute-start(bf16[1,64,128]{2,1,0:T(8,128)(2,1)S(1)} %get-tuple-element.5), channel_id=1, source_target_pairs={{0,14},{2,12},{4,10},{6,8},{8,6},{10,4},{12,2},{14,0},{1,15},{3,13... | collective-permute-start | bytes 49160 | tf_op jit(solution)/shard_map/ppermute | solution.py:18
  88.8 5.6 %copy-start.6 = (f32[8]{0:T(128)S(1)}, f32[8]{0:T(128)}, u32[]{:S(2)}) copy-start(f32[8]{0:T(128)} %param.13) | copy-start | bytes 100
  94.4 18.5 %copy-start.3 = (f32[16,1,4,8,1]{0,3,2,1,4:T(8,128)}, f32[16,1,4,8,1]{0,3,2,1,4:T(8,128)S(1)}, u32[]{:S(2)}) copy-start(f32[16,1,4,8,1]{0,3,2,1,4:T(8,128)S(1)} %copy.18) | copy-start | bytes 6148
Sparse Core Ops, SparseCore 0:
  50.3 17.8 all-reduce.2
